TPU v7x, 32 devices: a whole 2x2x4 slice. The times are simulated.
32 devices in a mesh: row: 8 (over y, x, core), col: 4 (over z).
Axes of the slice: x: 2, y: 2, z: 4, core: 2. Of those that a mesh axis runs over, the one named last changes fastest.
Arguments:
- emissions: float32 [2, 4, 1024, 512], P(None, None, 'row', 'col'), may hold values from 0 to 101
- winds: float32 [2, 2, 1024, 512], P(None, None, 'row', 'col'), may hold values from -0.4 to 0.4
- kernels: float32 [4, 65, 65], replicated, may hold values from 0 to 4
- box_states: float32 [4, 4, 1024, 512], P(None, None, 'row', 'col'), may hold values from 0.02 to 0.3
- decay: float32 [4, 4], replicated, may hold values from 0.3 to 0.95
- fraction: float32 [4, 4], replicated, may hold values from 0.1 to 0.6
Outputs:
- new_states: float32 [4, 4, 1024, 512], P(None, None, 'row', 'col')
- surface: float32 [4, 1024, 512], P(None, 'row', 'col')
All inputs are finite; a program needn't handle non-finite values.
Results may differ from a plain program's by a relative error of at most 0.0001.
Values sent between devices are 32-bit elements; how exact they have to be, the bound alone decides.
A program may use at most 64 MiB of HBM per device.

v0:
```python
import functools
import math

import jax
import jax.numpy as jnp
import numpy as np
from jax import lax
from jax.experimental import pallas as pl
from jax.experimental.pallas import tpu as pltpu
from jax.sharding import PartitionSpec as P

STEPS = 2
DIFFUSION = 0.05
MESH = pl.DeviceIdType.MESH
F32 = jnp.float32
BF16 = jnp.bfloat16


def split_table(table):
    high = table.astype(jnp.bfloat16)
    low = (table - high.astype(np.float64)).astype(jnp.bfloat16)
    return np.stack([high, low])


def tables(tile, reach, lanes):
    period = 2 * tile
    freq = (np.arange(tile) + 0.5) * (2.0 * math.pi / period)
    own = np.arange(tile)
    before = np.arange(-reach, 0)
    after = np.arange(tile, tile + reach)
    centred = np.arange(-reach, reach + 1)

    def forward_cols(positions):
        angle = positions[:, None] * freq[None, :]
        return np.concatenate([np.cos(angle), -np.sin(angle)], axis=1)

    def forward_rows(positions):
        angle = freq[:, None] * positions[None, :]
        return np.concatenate([np.cos(angle), np.sin(angle)], axis=0)

    cols_a = forward_cols(np.concatenate([own, before, before, after, after]))
    cols_b = forward_cols(np.concatenate([own, after, after, before, before]))
    rows_f = forward_rows(np.concatenate([own, before, after]))
    kernel_cols = np.zeros((lanes, 2 * tile))
    kernel_cols[: centred.size] = forward_cols(centred) * (2.0 / period**2)
    kernel_rows = np.zeros((2 * tile, lanes))
    kernel_rows[:, : centred.size] = forward_rows(centred)
    angle = own[:, None] * freq[None, :]
    rows_i = np.concatenate([np.cos(angle), np.sin(angle)], axis=1)
    cols_i = np.concatenate([np.cos(angle).T, -np.sin(angle).T], axis=0)
    return [split_table(t) for t in (cols_a, cols_b, rows_f, kernel_cols, kernel_rows, rows_i, cols_i)]


def split(value):
    high = value.astype(BF16)
    low = (value - high.astype(F32)).astype(BF16)
    return high, low


def dot3(left, right):
    lh, ll = left
    rh, rl = right
    return (
        jnp.dot(lh, rh, preferred_element_type=F32)
        + jnp.dot(ll, rh, preferred_element_type=F32)
        + jnp.dot(lh, rl, preferred_element_type=F32)
    )


def kernel(
    rows, cols, tile, reach,
    em, wd, kern, bs, decay, fraction,
    t_ca, t_cb, t_rf, t_ck, t_kr, t_ri, t_ci,
    out, surf,
    e_v, w_v, s_v,
    v_ca, v_cb, v_rf, v_ck, v_kr, v_ri, v_ci,
    kpad, kspec, send_e, send_w, west, east, ns, xh, xl, mix, src,
    n_send, s_send, n_recv, s_recv, c_send, w_recv, e_recv,
    coef,
    lsem, ssem, rsem,
):
    species = e_v.shape[1]
    boxes = s_v.shape[1]
    r = lax.axis_index("row")
    c = lax.axis_index("col")
    has = {"n": r > 0, "s": r < rows - 1, "w": c > 0, "e": c < cols - 1}
    dev = {
        "n": (jnp.maximum(r - 1, 0), c),
        "s": (jnp.minimum(r + 1, rows - 1), c),
        "w": (r, jnp.maximum(c - 1, 0)),
        "e": (r, jnp.minimum(c + 1, cols - 1)),
    }
    opposite = {"n": "s", "s": "n", "w": "e", "e": "w"}
    sends = []

    barrier = pltpu.get_barrier_semaphore()
    for side in "nswe":
        @pl.when(has[side])
        def _():
            pl.semaphore_signal(barrier, inc=1, device_id=dev[side], device_id_type=MESH)

    local = []

    def load(source, target):
        copy = pltpu.make_async_copy(source, target, lsem.at[len(local)])
        copy.start()
        local.append(copy)
        return copy

    load_e = [load(em.at[t], e_v.at[t]) for t in range(STEPS)]
    load_k = [load(a, b) for a, b in ((t_ck, v_ck), (t_kr, v_kr))]
    load_t = [
        load(a, b)
        for a, b in ((t_ca, v_ca), (t_cb, v_cb), (t_rf, v_rf), (t_ri, v_ri), (t_ci, v_ci))
    ]
    load_w = load(wd, w_v)
    load_s = load(bs, s_v)

    def remote(channel, side, source, target):
        return pltpu.make_async_remote_copy(
            src_ref=source,
            dst_ref=target,
            send_sem=ssem.at[channel],
            recv_sem=rsem.at[channel],
            device_id=dev[side],
            device_id_type=MESH,
        )

    def send(channel, side, source, target):
        @pl.when(has[side])
        def _():
            remote(channel, side, source, target).start()

        sends.append((channel, side, source, target))

    def wait_recv(channel, side, source, target):
        @pl.when(has[opposite[side]])
        def _():
            remote(channel, side, source, target).wait_recv()

    @pl.when(jnp.logical_not(has["n"]))
    def _():
        ns[:, :, :reach, :] = jnp.zeros((STEPS, species, reach, tile), F32)
        west[:, tile : tile + reach, :] = jnp.zeros((STEPS, reach, tile), F32)
        east[:, tile : tile + reach, :] = jnp.zeros((STEPS, reach, tile), F32)
        n_recv[...] = jnp.zeros(n_recv.shape, F32)

    @pl.when(jnp.logical_not(has["s"]))
    def _():
        ns[:, :, reach:, :] = jnp.zeros((STEPS, species, reach, tile), F32)
        west[:, tile + reach :, :] = jnp.zeros((STEPS, reach, tile), F32)
        east[:, tile + reach :, :] = jnp.zeros((STEPS, reach, tile), F32)
        s_recv[...] = jnp.zeros(s_recv.shape, F32)

    @pl.when(jnp.logical_not(has["w"]))
    def _():
        west[:, :tile, :] = jnp.zeros((STEPS, tile, tile), F32)
        w_recv[...] = jnp.zeros(w_recv.shape, F32)

    @pl.when(jnp.logical_not(has["e"]))
    def _():
        east[:, :tile, :] = jnp.zeros((STEPS, tile, tile), F32)
        e_recv[...] = jnp.zeros(e_recv.shape, F32)

    lane = lax.broadcasted_iota(jnp.int32, (tile, tile), 1)
    row = lax.broadcasted_iota(jnp.int32, (tile, tile), 0)
    slot = lane // reach
    own_rows = pl.ds(0, tile)

    def strip_args(t):
        return (
            (8 * t + 0, "e", send_e.at[t], west.at[t, own_rows]),
            (8 * t + 1, "w", send_w.at[t], east.at[t, own_rows]),
        )

    def row_args(t):
        return (
            (8 * t + 2, "s", em.at[t, :, pl.ds(tile - reach, reach), :], ns.at[t, :, pl.ds(0, reach), :]),
            (8 * t + 3, "n", em.at[t, :, pl.ds(0, reach), :], ns.at[t, :, pl.ds(reach, reach), :]),
        )

    def corner_args(t):
        found = []
        for position, strip in enumerate((west, east)):
            found.append(
                (8 * t + 4 + 2 * position, "s", strip.at[t, pl.ds(tile - reach, reach)], strip.at[t, pl.ds(tile, reach)])
            )
            found.append(
                (8 * t + 5 + 2 * position, "n", strip.at[t, pl.ds(0, reach)], strip.at[t, pl.ds(tile + reach, reach)])
            )
        return found

    for t in range(STEPS):
        load_e[t].wait()
        for target, first, turn in ((send_e, tile - reach, 0), (send_w, 0, 2)):
            packed = None
            for s in range(species):
                place = (s + turn) % species
                moved = pltpu.roll(e_v[t, s], (reach * place - first) % tile, 1)
                packed = moved if packed is None else jnp.where(slot == place, moved, packed)
            target[t] = packed
        if t == 0:
            peers = sum(has[side].astype(jnp.int32) for side in "nswe")
            pl.semaphore_wait(barrier, peers)
        for args in strip_args(t) + row_args(t):
            send(*args)

    kpad[...] = jnp.zeros(kpad.shape, F32)
    width = 2 * reach + 1
    for s in range(species):
        kpad[s, :width, :width] = kern[:, s, :]
    for copy in load_k:
        copy.wait()
    def even_odd(value):
        u, w = value[:tile, :tile], value[:tile, tile:]
        z, v = value[tile:, :tile], value[tile:, tile:]
        return u + v, w - z, u - v, w + z

    for s in range(species):
        first = dot3(split(kpad[s]), (v_ck[0], v_ck[1]))
        second = dot3((v_kr[0], v_kr[1]), split(first))
        for position, value in enumerate(even_odd(second)):
            kspec[s, position] = value

    def own_part(t):
        for s in range(species):
            high, low = split(e_v[t, s])
            xh[s, :tile, :tile] = high
            xl[s, :tile, :tile] = low

    def rows_part(t):
        for s in range(species):
            high, low = split(ns[t, s])
            xh[s, tile:, :tile] = high
            xl[s, tile:, :tile] = low

    def cols_part(t):
        wide = lax.broadcasted_iota(jnp.int32, (tile + 2 * reach, tile), 1)
        from_west, from_east = west[t], east[t]
        left = wide < tile // 2
        for pair in range(2):
            joined = jnp.where(left, from_west, from_east) if pair == 0 else jnp.where(left, from_east, from_west)
            for odd in range(2):
                s = 2 * pair + odd
                mine = jnp.where((wide // reach) % 2 == odd, joined, 0.0)
                high, low = split(mine)
                xh[s, :, tile:] = high
                xl[s, :, tile:] = low

    def disperse(t):
        for s in range(species):
            table = v_ca if s < 2 else v_cb
            a = dot3((xh[s], xl[s]), (table[0], table[1]))
            b = dot3((v_rf[0], v_rf[1]), split(a))
            pr, pi, mr, mi = even_odd(b)
            kpr, kpi, kmr, kmi = (kspec[s, n] for n in range(4))
            gpr = pr * kpr - pi * kpi
            gpi = pr * kpi + pi * kpr
            gmr = mr * kmr - mi * kmi
            gmi = mr * kmi + mi * kmr
            top = jnp.concatenate([gpr + gmr, gpi + gmi], axis=1)
            bottom = jnp.concatenate([gmi - gpi, gpr - gmr], axis=1)
            g = jnp.concatenate([top, bottom], axis=0)
            d = dot3((v_ri[0], v_ri[1]), split(g))
            src[t, s] = dot3(split(d), (v_ci[0], v_ci[1]))

    first_row = 8
    inner = pl.ds(first_row, tile)
    packed_rows = c_send.shape[1]

    def edge_args(t):
        base = 16 + 4 * t
        return (
            (base + 0, "n", n_send.at[t], s_recv.at[t]),
            (base + 1, "s", s_send.at[t], n_recv.at[t]),
            (base + 2, "w", c_send.at[t], e_recv.at[t]),
            (base + 3, "e", c_send.at[t], w_recv.at[t]),
        )

    def mix_and_send(t, state):
        packed = jnp.zeros((tile, tile), F32)
        for s in range(species):
            for k in range(boxes):
                f = s * boxes + k
                m = decay[s, k] * state[s, k] + fraction[s, k] * src[t, s]
                mix[f, inner, :] = m
                n_send[t, f : f + 1, :] = m[0:1, :]
                s_send[t, f : f + 1, :] = m[tile - 1 : tile, :]
                packed = jnp.where(lane // 2 == f, pltpu.roll(m, 2 * f + 1, 1), packed)
        c_send[t] = packed.T[:packed_rows]
        for args in edge_args(t):
            send(*args)

    def coefficients(t):
        u, v = w_v[t, 0], w_v[t, 1]
        up, um = jnp.maximum(u, 0.0), jnp.minimum(u, 0.0)
        vp, vm = jnp.maximum(v, 0.0), jnp.minimum(v, 0.0)
        coef[0] = (1.0 - 4.0 * DIFFUSION) - up + um - vp + vm
        to_west, to_east = up + DIFFUSION, DIFFUSION - um
        coef[1] = jnp.where(lane > 0, to_west, 0.0)
        coef[2] = jnp.where(lane < tile - 1, to_east, 0.0)
        coef[3] = vp + DIFFUSION
        coef[4] = DIFFUSION - vm
        coef[5] = jnp.where(lane == 0, to_west, jnp.where(lane == tile - 1, to_east, 0.0))

    def transport(t, result):
        for args in edge_args(t):
            wait_recv(*args)
        for f in range(species * boxes):
            mix[f, first_row - 1 : first_row, :] = n_recv[t, f : f + 1, :]
            mix[f, first_row + tile : first_row + tile + 1, :] = s_recv[t, f : f + 1, :]
        odd = lax.broadcasted_iota(jnp.int32, (packed_rows, tile), 0) % 2 == 1
        joined = jnp.where(
            odd, pltpu.roll(w_recv[t], 1, 0), pltpu.roll(e_recv[t], packed_rows - 1, 0)
        )
        joined = jnp.concatenate([joined, jnp.zeros((tile - packed_rows, tile), F32)], axis=0)
        beside = joined.T
        for s in range(species):
            total = None
            for k in range(boxes):
                f = s * boxes + k
                m = mix[f, inner, :]
                value = (
                    coef[0] * m
                    + coef[1] * pltpu.roll(m, 1, 1)
                    + coef[2] * pltpu.roll(m, tile - 1, 1)
                    + coef[3] * mix[f, pl.ds(first_row - 1, tile), :]
                    + coef[4] * mix[f, pl.ds(first_row + 1, tile), :]
                    + coef[5] * pltpu.roll(beside, (tile - 2 * f - 1) % tile, 1)
                )
                result[s, k] = value
                total = value if total is None else total + value
            if t == STEPS - 1:
                surf[s] = total

    def arrive(t):
        for args in strip_args(t):
            wait_recv(*args)
        for args in corner_args(t):
            send(*args)

    def source(t):
        own_part(t)
        for args in row_args(t):
            wait_recv(*args)
        rows_part(t)
        for args in corner_args(t):
            wait_recv(*args)
        cols_part(t)
        disperse(t)

    arrive(0)
    for copy in load_t:
        copy.wait()
    source(0)
    arrive(1)
    load_s.wait()
    load_w.wait()
    mix_and_send(0, s_v)
    source(1)
    coefficients(0)
    transport(0, s_v)
    mix_and_send(1, s_v)
    coefficients(1)
    transport(1, out)
    for channel, side, sent, target in sends:
        @pl.when(has[side])
        def _():
            remote(channel, side, sent, target).wait_send()


def on_device(rows, cols, emissions, winds, kernels, box_states, decay, fraction):
    _, species, tile, _ = emissions.shape
    boxes = box_states.shape[1]
    reach = (kernels.shape[-1] - 1) // 2
    fields = species * boxes
    tabs = [jnp.asarray(t) for t in tables(tile, reach, tile)]
    hbm = pl.BlockSpec(memory_space=pltpu.HBM)
    vmem = pl.BlockSpec(memory_space=pltpu.VMEM)
    smem = pl.BlockSpec(memory_space=pltpu.SMEM)
    span = tile + 2 * reach

    def buf(*shape, dtype=F32):
        return pltpu.VMEM(shape, dtype)

    channels = 16 + 4 * STEPS
    return tuple(
        pl.pallas_call(
            functools.partial(kernel, rows, cols, tile, reach),
            out_shape=(
                jax.ShapeDtypeStruct(box_states.shape, F32),
                jax.ShapeDtypeStruct((species, tile, tile), F32),
            ),
            in_specs=[hbm, hbm, vmem, hbm, smem, smem] + [hbm] * len(tabs),
            out_specs=(vmem, vmem),
            scratch_shapes=[
                buf(STEPS, species, tile, tile),
                buf(STEPS, 2, tile, tile),
                buf(species, boxes, tile, tile),
            ]
            + [buf(*t.shape, dtype=BF16) for t in tabs]
            + [
                buf(species, tile, tile),
                buf(species, 4, tile, tile),
                buf(STEPS, tile, tile),
                buf(STEPS, tile, tile),
                buf(STEPS, span, tile),
                buf(STEPS, span, tile),
                buf(STEPS, species, 2 * reach, tile),
                buf(species, span, 2 * tile, dtype=BF16),
                buf(species, span, 2 * tile, dtype=BF16),
                buf(fields, tile + 16, tile),
                buf(STEPS, species, tile, tile),
                buf(STEPS, fields, tile),
                buf(STEPS, fields, tile),
                buf(STEPS, fields, tile),
                buf(STEPS, fields, tile),
                buf(STEPS, 2 * fields, tile),
                buf(STEPS, 2 * fields, tile),
                buf(STEPS, 2 * fields, tile),
                buf(6, tile, tile),
                pltpu.SemaphoreType.DMA((STEPS + len(tabs) + 2,)),
                pltpu.SemaphoreType.DMA((channels,)),
                pltpu.SemaphoreType.DMA((channels,)),
            ],
            compiler_params=pltpu.CompilerParams(
                collective_id=0, has_side_effects=True, vmem_limit_bytes=61 * 2**20
            ),
        )(emissions, winds, kernels.transpose(1, 0, 2), box_states, decay, fraction, *tabs)
    )


def solution(mesh):
    placed = (
        P(None, None, "row", "col"),
        P(None, None, "row", "col"),
        P(),
        P(None, None, "row", "col"),
        P(),
        P(),
    )
    return jax.shard_map(
        functools.partial(on_device, mesh.shape["row"], mesh.shape["col"]),
        mesh=mesh,
        in_specs=placed,
        out_specs=(P(None, None, "row", "col"), P(None, "row", "col")),
        check_vma=False,
    )
```

profile of v0, /device:TPU:1, one launch (start us, length us, event | category | flops | bytes accessed | tf_op | source)
XLA Modules:
  0.0 31.1 jit_solution(18310313776262722672)
XLA Ops:
  0.6 27.4 %shard_map.140 = (f32[4,4,128,128]{3,2,1,0:T(8,128)}, f32[4,128,128]{2,1,0:T(8,128)}) custom-call(f32[2,4,128,128]{3,2,1,0:T(8,128)} %em.1, f32[2,2,128,128]{3,2,1,0:T(8,128)} %wd.1, f32[65,4,65]{2,1,0:T(4,128)} %bitcast.1, f32[4,4,128,128]{3,2,1,0:T(8,128)} %bs.1, f32[4,4]{1,0:T(4,128)} %decay.1, f32[4,4]{1,0:T(4,128)} %fraction.1, ...), custom_call_target="tpu_custom_call" | custom-call | tf_op jit(solution)/shard_map/pallas_call | solution.py:388
  28.0 0.0 copy-start
  28.1 2.3 %copy.17 = f32[4,4,128,128]{3,2,1,0:T(8,128)} copy(f32[4,4,128,128]{3,2,1,0:T(8,128)} %get-tuple-element.4) | data formatting | bytes 2097152
  30.4 0.0 copy-done
  30.4 0.7 %copy.18 = f32[4,128,128]{2,1,0:T(8,128)} copy(f32[4,128,128]{2,1,0:T(8,128)S(1)} %copy-done) | data formatting | bytes 524288
Async XLA Ops:
  28.0 2.4 %copy-start = (f32[4,128,128]{2,1,0:T(8,128)S(1)}, f32[4,128,128]{2,1,0:T(8,128)}, u32[]{:S(2)}) copy-start(f32[4,128,128]{2,1,0:T(8,128)} %get-tuple-element.5) | copy-start | bytes 786436
where the time goes:
time: 31.5 us; the launch traced here: 31.1 us
  Pallas kernels  27.4 us (87%)
  local copies, waits for them, and re-layouts  3.04 us (10%)
  between operations  0.65 us (2%)
    pallas_call x1, Pallas kernels, on_device(): pl.pallas_call(functools.partial(kernel, rows, cols, tile, reach), out_sh...  27.4 us
    unnamed x4, local copies, waits for them, and re-layouts  3.04 us

commit v1 on v0

--- a/solution.py
+++ b/solution.py
@@ -72,7 +72,7 @@
     em, wd, kern, bs, decay, fraction,
     t_ca, t_cb, t_rf, t_ck, t_kr, t_ri, t_ci,
     out, surf,
-    e_v, w_v, s_v,
+    e_v, w_v, s_v, k_v,
     v_ca, v_cb, v_rf, v_ck, v_kr, v_ri, v_ci,
     kpad, kspec, send_e, send_w, west, east, ns, xh, xl, mix, src,
     n_send, s_send, n_recv, s_recv, c_send, w_recv, e_recv,
@@ -84,17 +84,17 @@
     r = lax.axis_index("row")
     c = lax.axis_index("col")
     has = {"n": r > 0, "s": r < rows - 1, "w": c > 0, "e": c < cols - 1}
-    dev = {
-        "n": (jnp.maximum(r - 1, 0), c),
-        "s": (jnp.minimum(r + 1, rows - 1), c),
-        "w": (r, jnp.maximum(c - 1, 0)),
-        "e": (r, jnp.minimum(c + 1, cols - 1)),
-    }
-    opposite = {"n": "s", "s": "n", "w": "e", "e": "w"}
+    up, down = jnp.maximum(r - 1, 0), jnp.minimum(r + 1, rows - 1)
+    left, right = jnp.maximum(c - 1, 0), jnp.minimum(c + 1, cols - 1)
+    dev = {"n": (up, c), "s": (down, c), "w": (r, left), "e": (r, right)}
+    dev |= {"nw": (up, left), "ne": (up, right), "sw": (down, left), "se": (down, right)}
+    for side in ("nw", "ne", "sw", "se"):
+        has[side] = jnp.logical_and(has[side[0]], has[side[1]])
+    opposite = {"n": "s", "s": "n", "w": "e", "e": "w", "nw": "se", "se": "nw", "ne": "sw", "sw": "ne"}
     sends = []
 
     barrier = pltpu.get_barrier_semaphore()
-    for side in "nswe":
+    for side in has:
         @pl.when(has[side])
         def _():
             pl.semaphore_signal(barrier, inc=1, device_id=dev[side], device_id_type=MESH)
@@ -108,7 +108,7 @@
         return copy
 
     load_e = [load(em.at[t], e_v.at[t]) for t in range(STEPS)]
-    load_k = [load(a, b) for a, b in ((t_ck, v_ck), (t_kr, v_kr))]
+    load_k = [load(a, b) for a, b in ((kern, k_v), (t_ck, v_ck), (t_kr, v_kr))]
     load_t = [
         load(a, b)
         for a, b in ((t_ca, v_ca), (t_cb, v_cb), (t_rf, v_rf), (t_ri, v_ri), (t_ci, v_ci))
@@ -141,15 +141,11 @@
     @pl.when(jnp.logical_not(has["n"]))
     def _():
         ns[:, :, :reach, :] = jnp.zeros((STEPS, species, reach, tile), F32)
-        west[:, tile : tile + reach, :] = jnp.zeros((STEPS, reach, tile), F32)
-        east[:, tile : tile + reach, :] = jnp.zeros((STEPS, reach, tile), F32)
         n_recv[...] = jnp.zeros(n_recv.shape, F32)
 
     @pl.when(jnp.logical_not(has["s"]))
     def _():
         ns[:, :, reach:, :] = jnp.zeros((STEPS, species, reach, tile), F32)
-        west[:, tile + reach :, :] = jnp.zeros((STEPS, reach, tile), F32)
-        east[:, tile + reach :, :] = jnp.zeros((STEPS, reach, tile), F32)
         s_recv[...] = jnp.zeros(s_recv.shape, F32)
 
     @pl.when(jnp.logical_not(has["w"]))
@@ -162,6 +158,13 @@
         east[:, :tile, :] = jnp.zeros((STEPS, tile, tile), F32)
         e_recv[...] = jnp.zeros(e_recv.shape, F32)
 
+    for side, strip, first in (
+        ("nw", west, tile), ("sw", west, tile + reach), ("ne", east, tile), ("se", east, tile + reach)
+    ):
+        @pl.when(jnp.logical_not(has[side]))
+        def _():
+            strip[:, first : first + reach, :] = jnp.zeros((STEPS, reach, tile), F32)
+
     lane = lax.broadcasted_iota(jnp.int32, (tile, tile), 1)
     row = lax.broadcasted_iota(jnp.int32, (tile, tile), 0)
     slot = lane // reach
@@ -180,15 +183,14 @@
         )
 
     def corner_args(t):
-        found = []
-        for position, strip in enumerate((west, east)):
-            found.append(
-                (8 * t + 4 + 2 * position, "s", strip.at[t, pl.ds(tile - reach, reach)], strip.at[t, pl.ds(tile, reach)])
-            )
-            found.append(
-                (8 * t + 5 + 2 * position, "n", strip.at[t, pl.ds(0, reach)], strip.at[t, pl.ds(tile + reach, reach)])
-            )
-        return found
+        top, bottom = pl.ds(0, reach), pl.ds(tile - reach, reach)
+        before, after = pl.ds(tile, reach), pl.ds(tile + reach, reach)
+        return (
+            (8 * t + 4, "se", send_e.at[t, bottom], west.at[t, before]),
+            (8 * t + 5, "ne", send_e.at[t, top], west.at[t, after]),
+            (8 * t + 6, "sw", send_w.at[t, bottom], east.at[t, before]),
+            (8 * t + 7, "nw", send_w.at[t, top], east.at[t, after]),
+        )
 
     for t in range(STEPS):
         load_e[t].wait()
@@ -200,17 +202,17 @@
                 packed = moved if packed is None else jnp.where(slot == place, moved, packed)
             target[t] = packed
         if t == 0:
-            peers = sum(has[side].astype(jnp.int32) for side in "nswe")
+            peers = sum(has[side].astype(jnp.int32) for side in has)
             pl.semaphore_wait(barrier, peers)
-        for args in strip_args(t) + row_args(t):
+        for args in strip_args(t) + corner_args(t) + row_args(t):
             send(*args)
 
     kpad[...] = jnp.zeros(kpad.shape, F32)
     width = 2 * reach + 1
-    for s in range(species):
-        kpad[s, :width, :width] = kern[:, s, :]
     for copy in load_k:
         copy.wait()
+    for s in range(species):
+        kpad[s, :width, :width] = k_v[:, s, :]
     def even_odd(value):
         u, w = value[:tile, :tile], value[:tile, tile:]
         z, v = value[tile:, :tile], value[tile:, tile:]
@@ -248,11 +250,17 @@
                 xl[s, :, tile:] = low
 
     def disperse(t):
-        for s in range(species):
-            table = v_ca if s < 2 else v_cb
-            a = dot3((xh[s], xl[s]), (table[0], table[1]))
-            b = dot3((v_rf[0], v_rf[1]), split(a))
-            pr, pi, mr, mi = even_odd(b)
+        span = tile + 2 * reach
+        firsts = []
+        for pair, table in enumerate((v_ca, v_cb)):
+            both = pl.ds(2 * pair, 2)
+            x = tuple(ref[both].reshape(2 * span, 2 * tile) for ref in (xh, xl))
+            a = dot3(x, (table[0], table[1]))
+            firsts += [split(a[:span]), split(a[span:])]
+        seconds = [dot3((v_rf[0], v_rf[1]), a) for a in firsts]
+        spectra = []
+        for s in range(species):
+            pr, pi, mr, mi = even_odd(seconds[s])
             kpr, kpi, kmr, kmi = (kspec[s, n] for n in range(4))
             gpr = pr * kpr - pi * kpi
             gpi = pr * kpi + pi * kpr
@@ -260,9 +268,10 @@
             gmi = mr * kmi + mi * kmr
             top = jnp.concatenate([gpr + gmr, gpi + gmi], axis=1)
             bottom = jnp.concatenate([gmi - gpi, gpr - gmr], axis=1)
-            g = jnp.concatenate([top, bottom], axis=0)
-            d = dot3((v_ri[0], v_ri[1]), split(g))
-            src[t, s] = dot3(split(d), (v_ci[0], v_ci[1]))
+            spectra.append(split(jnp.concatenate([top, bottom], axis=0)))
+        thirds = [split(dot3((v_ri[0], v_ri[1]), g)) for g in spectra]
+        for s in range(species):
+            src[t, s] = dot3(thirds[s], (v_ci[0], v_ci[1]))
 
     first_row = 8
     inner = pl.ds(first_row, tile)
@@ -303,66 +312,79 @@
         coef[4] = DIFFUSION - vm
         coef[5] = jnp.where(lane == 0, to_west, jnp.where(lane == tile - 1, to_east, 0.0))
 
-    def transport(t, result):
+    def stencil(f):
+        m = mix[f, inner, :]
+        return (
+            coef[0] * m
+            + coef[1] * pltpu.roll(m, 1, 1)
+            + coef[2] * pltpu.roll(m, tile - 1, 1)
+            + coef[3] * mix[f, pl.ds(first_row - 1, tile), :]
+            + coef[4] * mix[f, pl.ds(first_row + 1, tile), :]
+        )
+
+    def beside(t):
+        odd = lax.broadcasted_iota(jnp.int32, (packed_rows, tile), 0) % 2 == 1
+        joined = jnp.where(
+            odd, pltpu.roll(w_recv[t], 1, 0), pltpu.roll(e_recv[t], packed_rows - 1, 0)
+        )
+        return jnp.concatenate([joined, jnp.zeros((tile - packed_rows, tile), F32)], axis=0).T
+
+    def from_sides(halo, f):
+        return coef[5] * pltpu.roll(halo, (tile - 2 * f - 1) % tile, 1)
+
+    def transport_first(t, result):
         for args in edge_args(t):
             wait_recv(*args)
         for f in range(species * boxes):
             mix[f, first_row - 1 : first_row, :] = n_recv[t, f : f + 1, :]
             mix[f, first_row + tile : first_row + tile + 1, :] = s_recv[t, f : f + 1, :]
-        odd = lax.broadcasted_iota(jnp.int32, (packed_rows, tile), 0) % 2 == 1
-        joined = jnp.where(
-            odd, pltpu.roll(w_recv[t], 1, 0), pltpu.roll(e_recv[t], packed_rows - 1, 0)
-        )
-        joined = jnp.concatenate([joined, jnp.zeros((tile - packed_rows, tile), F32)], axis=0)
-        beside = joined.T
-        for s in range(species):
-            total = None
+        halo = beside(t)
+        for f in range(species * boxes):
+            result[f // boxes, f % boxes] = stencil(f) + from_sides(halo, f)
+
+    def transport_last(t, result, total):
+        north, south = coef[3, 0:1, :], coef[4, tile - 1 : tile, :]
+        coef[3] = jnp.where(row > 0, coef[3], 0.0)
+        coef[4] = jnp.where(row < tile - 1, coef[4], 0.0)
+        for f in range(species * boxes):
+            result[f // boxes, f % boxes] = stencil(f)
+        for args in edge_args(t):
+            wait_recv(*args)
+        halo = beside(t)
+        for s in range(species):
             for k in range(boxes):
                 f = s * boxes + k
-                m = mix[f, inner, :]
-                value = (
-                    coef[0] * m
-                    + coef[1] * pltpu.roll(m, 1, 1)
-                    + coef[2] * pltpu.roll(m, tile - 1, 1)
-                    + coef[3] * mix[f, pl.ds(first_row - 1, tile), :]
-                    + coef[4] * mix[f, pl.ds(first_row + 1, tile), :]
-                    + coef[5] * pltpu.roll(beside, (tile - 2 * f - 1) % tile, 1)
-                )
+                result[s, k, 0:1, :] += north * n_recv[t, f : f + 1, :]
+                result[s, k, tile - 1 : tile, :] += south * s_recv[t, f : f + 1, :]
+            summed = None
+            for k in range(boxes):
+                value = result[s, k] + from_sides(halo, s * boxes + k)
                 result[s, k] = value
-                total = value if total is None else total + value
-            if t == STEPS - 1:
-                surf[s] = total
-
-    def arrive(t):
-        for args in strip_args(t):
-            wait_recv(*args)
-        for args in corner_args(t):
-            send(*args)
+                summed = value if summed is None else summed + value
+            total[s] = summed
 
     def source(t):
         own_part(t)
         for args in row_args(t):
             wait_recv(*args)
         rows_part(t)
-        for args in corner_args(t):
+        for args in strip_args(t) + corner_args(t):
             wait_recv(*args)
         cols_part(t)
         disperse(t)
 
-    arrive(0)
     for copy in load_t:
         copy.wait()
     source(0)
-    arrive(1)
     load_s.wait()
     load_w.wait()
     mix_and_send(0, s_v)
     source(1)
     coefficients(0)
-    transport(0, s_v)
+    transport_first(0, s_v)
     mix_and_send(1, s_v)
     coefficients(1)
-    transport(1, out)
+    transport_last(1, out, surf)
     for channel, side, sent, target in sends:
         @pl.when(has[side])
         def _():
@@ -391,12 +413,13 @@
                 jax.ShapeDtypeStruct(box_states.shape, F32),
                 jax.ShapeDtypeStruct((species, tile, tile), F32),
             ),
-            in_specs=[hbm, hbm, vmem, hbm, smem, smem] + [hbm] * len(tabs),
+            in_specs=[hbm, hbm, hbm, hbm, smem, smem] + [hbm] * len(tabs),
             out_specs=(vmem, vmem),
             scratch_shapes=[
                 buf(STEPS, species, tile, tile),
                 buf(STEPS, 2, tile, tile),
                 buf(species, boxes, tile, tile),
+                buf(2 * reach + 1, species, 2 * reach + 1),
             ]
             + [buf(*t.shape, dtype=BF16) for t in tabs]
             + [
@@ -419,7 +442,7 @@
                 buf(STEPS, 2 * fields, tile),
                 buf(STEPS, 2 * fields, tile),
                 buf(6, tile, tile),
-                pltpu.SemaphoreType.DMA((STEPS + len(tabs) + 2,)),
+                pltpu.SemaphoreType.DMA((STEPS + len(tabs) + 3,)),
                 pltpu.SemaphoreType.DMA((channels,)),
                 pltpu.SemaphoreType.DMA((channels,)),
             ],

time: 31.5 us -> 24.5 us (0.78)
  Pallas kernels: 27.4 us -> 20.6 us
    pallas_call x1, Pallas kernels: 27.4 us -> 20.6 us  [on_device(): pl.pallas_call(functools.partial(kernel, rows, cols, tile, reach), out_sh...]
where the time goes in v1:
time: 24.5 us; the launch traced here: 24.3 us
  Pallas kernels  20.6 us (84%)
  local copies, waits for them, and re-layouts  3.04 us (12%)
  between operations  0.65 us (3%)
    pallas_call x1, Pallas kernels, on_device(): pl.pallas_call(functools.partial(kernel, rows, cols, tile, reach), out_sh...  20.6 us
    unnamed x4, local copies, waits for them, and re-layouts  3.04 us

profile of v1, /device:TPU:1, one launch (start us, length us, event | category | flops | bytes accessed | tf_op | source)
XLA Modules:
  0.0 24.3 jit_solution(7833287186633511188)
XLA Ops:
  0.6 20.6 %shard_map.140 = (f32[4,4,128,128]{3,2,1,0:T(8,128)}, f32[4,128,128]{2,1,0:T(8,128)}) custom-call(f32[2,4,128,128]{3,2,1,0:T(8,128)} %em.1, f32[2,2,128,128]{3,2,1,0:T(8,128)} %wd.1, f32[65,4,65]{2,1,0:T(4,128)} %bitcast.1, f32[4,4,128,128]{3,2,1,0:T(8,128)} %bs.1, f32[4,4]{1,0:T(4,128)} %decay.1, f32[4,4]{1,0:T(4,128)} %fraction.1, ...), custom_call_target="tpu_custom_call" | custom-call | tf_op jit(solution)/shard_map/pallas_call | solution.py:410
  21.3 0.0 copy-start
  21.3 2.3 %copy.17 = f32[4,4,128,128]{3,2,1,0:T(8,128)} copy(f32[4,4,128,128]{3,2,1,0:T(8,128)} %get-tuple-element.4) | data formatting | bytes 2097152
  23.6 0.0 copy-done
  23.6 0.7 %copy.18 = f32[4,128,128]{2,1,0:T(8,128)} copy(f32[4,128,128]{2,1,0:T(8,128)S(1)} %copy-done) | data formatting | bytes 524288
Async XLA Ops:
  21.3 2.4 %copy-start = (f32[4,128,128]{2,1,0:T(8,128)S(1)}, f32[4,128,128]{2,1,0:T(8,128)}, u32[]{:S(2)}) copy-start(f32[4,128,128]{2,1,0:T(8,128)} %get-tuple-element.5) | copy-start | bytes 786436

commit v2 on v1

--- a/solution.py
+++ b/solution.py
@@ -71,13 +71,13 @@
     rows, cols, tile, reach,
     em, wd, kern, bs, decay, fraction,
     t_ca, t_cb, t_rf, t_ck, t_kr, t_ri, t_ci,
-    out, surf,
-    e_v, w_v, s_v, k_v,
+    part, side_halo, side_coef, row_halo,
+    e_v, w_v, s_v, o_v, k_v,
     v_ca, v_cb, v_rf, v_ck, v_kr, v_ri, v_ci,
     kpad, kspec, send_e, send_w, west, east, ns, xh, xl, mix, src,
     n_send, s_send, n_recv, s_recv, c_send, w_recv, e_recv,
     coef,
-    lsem, ssem, rsem,
+    lsem, ssem, rsem, osem,
 ):
     species = e_v.shape[1]
     boxes = s_v.shape[1]
@@ -342,26 +342,22 @@
         for f in range(species * boxes):
             result[f // boxes, f % boxes] = stencil(f) + from_sides(halo, f)
 
-    def transport_last(t, result, total):
+    def transport_last(t):
         north, south = coef[3, 0:1, :], coef[4, tile - 1 : tile, :]
         coef[3] = jnp.where(row > 0, coef[3], 0.0)
         coef[4] = jnp.where(row < tile - 1, coef[4], 0.0)
-        for f in range(species * boxes):
-            result[f // boxes, f % boxes] = stencil(f)
+        side_coef[...] = coef[5]
+        for s in range(species):
+            for k in range(boxes):
+                o_v[s, k] = stencil(s * boxes + k)
+            pltpu.make_async_copy(o_v.at[s], part.at[s], osem.at[s]).start()
         for args in edge_args(t):
             wait_recv(*args)
-        halo = beside(t)
-        for s in range(species):
-            for k in range(boxes):
-                f = s * boxes + k
-                result[s, k, 0:1, :] += north * n_recv[t, f : f + 1, :]
-                result[s, k, tile - 1 : tile, :] += south * s_recv[t, f : f + 1, :]
-            summed = None
-            for k in range(boxes):
-                value = result[s, k] + from_sides(halo, s * boxes + k)
-                result[s, k] = value
-                summed = value if summed is None else summed + value
-            total[s] = summed
+        side_halo[...] = beside(t)
+        for s in range(species):
+            fields = slice(s * boxes, (s + 1) * boxes)
+            row_halo[0, s] = north * n_recv[t, fields, :]
+            row_halo[1, s] = south * s_recv[t, fields, :]
 
     def source(t):
         own_part(t)
@@ -384,11 +380,44 @@
     transport_first(0, s_v)
     mix_and_send(1, s_v)
     coefficients(1)
-    transport_last(1, out, surf)
+    transport_last(1)
     for channel, side, sent, target in sends:
         @pl.when(has[side])
         def _():
             remote(channel, side, sent, target).wait_send()
+    for s in range(species):
+        pltpu.make_async_copy(o_v.at[s], part.at[s], osem.at[s]).wait()
+
+
+def finish(tile, part, side_halo, side_coef, row_halo, out, surf, p_v, h_v, c_v, r_v, f_v, isem, osem):
+    species, boxes = part.shape[:2]
+    pairs = [(side_halo, h_v), (side_coef, c_v), (row_halo, r_v)]
+    pairs += [(part.at[s], p_v.at[s]) for s in range(species)]
+    loads = [pltpu.make_async_copy(a, b, isem.at[n]) for n, (a, b) in enumerate(pairs)]
+    for copy in loads:
+        copy.start()
+    for copy in loads[:3]:
+        copy.wait()
+    stores = []
+    for s in range(species):
+        loads[3 + s].wait()
+        summed = None
+        for k in range(boxes):
+            turn = (tile - 2 * (s * boxes + k) - 1) % tile
+            value = p_v[s, k] + c_v[...] * pltpu.roll(h_v[...], turn, 1)
+            p_v[s, k] = value
+            p_v[s, k, 0:1] += r_v[0, s, k : k + 1]
+            p_v[s, k, tile - 1 :] += r_v[1, s, k : k + 1]
+            summed = value if summed is None else summed + value
+        f_v[s] = summed
+        f_v[s, 0:1] += jnp.sum(r_v[0, s], axis=0, keepdims=True)
+        f_v[s, tile - 1 :] += jnp.sum(r_v[1, s], axis=0, keepdims=True)
+        stores.append(pltpu.make_async_copy(p_v.at[s], out.at[s], osem.at[2 * s]))
+        stores.append(pltpu.make_async_copy(f_v.at[s], surf.at[s], osem.at[2 * s + 1]))
+        for copy in stores[-2:]:
+            copy.start()
+    for copy in stores:
+        copy.wait()
 
 
 def on_device(rows, cols, emissions, winds, kernels, box_states, decay, fraction):
@@ -406,18 +435,21 @@
         return pltpu.VMEM(shape, dtype)
 
     channels = 16 + 4 * STEPS
-    return tuple(
+    partial = tuple(
         pl.pallas_call(
             functools.partial(kernel, rows, cols, tile, reach),
             out_shape=(
                 jax.ShapeDtypeStruct(box_states.shape, F32),
-                jax.ShapeDtypeStruct((species, tile, tile), F32),
+                jax.ShapeDtypeStruct((tile, tile), F32),
+                jax.ShapeDtypeStruct((tile, tile), F32),
+                jax.ShapeDtypeStruct((2, species, boxes, tile), F32),
             ),
             in_specs=[hbm, hbm, hbm, hbm, smem, smem] + [hbm] * len(tabs),
-            out_specs=(vmem, vmem),
+            out_specs=(hbm, vmem, vmem, vmem),
             scratch_shapes=[
                 buf(STEPS, species, tile, tile),
                 buf(STEPS, 2, tile, tile),
+                buf(species, boxes, tile, tile),
                 buf(species, boxes, tile, tile),
                 buf(2 * reach + 1, species, 2 * reach + 1),
             ]
@@ -445,11 +477,33 @@
                 pltpu.SemaphoreType.DMA((STEPS + len(tabs) + 3,)),
                 pltpu.SemaphoreType.DMA((channels,)),
                 pltpu.SemaphoreType.DMA((channels,)),
+                pltpu.SemaphoreType.DMA((species,)),
             ],
             compiler_params=pltpu.CompilerParams(
                 collective_id=0, has_side_effects=True, vmem_limit_bytes=61 * 2**20
             ),
         )(emissions, winds, kernels.transpose(1, 0, 2), box_states, decay, fraction, *tabs)
+    )
+    return tuple(
+        pl.pallas_call(
+            functools.partial(finish, tile),
+            out_shape=(
+                jax.ShapeDtypeStruct(box_states.shape, F32),
+                jax.ShapeDtypeStruct((species, tile, tile), F32),
+            ),
+            in_specs=[hbm] * 4,
+            out_specs=(hbm, hbm),
+            scratch_shapes=[
+                buf(species, boxes, tile, tile),
+                buf(tile, tile),
+                buf(tile, tile),
+                buf(2, species, boxes, tile),
+                buf(species, tile, tile),
+                pltpu.SemaphoreType.DMA((3 + species,)),
+                pltpu.SemaphoreType.DMA((2 * species,)),
+            ],
+            compiler_params=pltpu.CompilerParams(vmem_limit_bytes=61 * 2**20),
+        )(*partial)
     )
 
 

time: 24.5 us -> 23.2 us (0.947)
  local copies, waits for them, and re-layouts: 3.04 us -> 0 us
  Pallas kernels: 20.6 us -> 22.4 us
    unnamed x4 -> x0, local copies, waits for them, and re-layouts: 3.04 us -> none
    pallas_call x0 -> x1, Pallas kernels: none -> 2.47 us  [on_device(): pl.pallas_call(functools.partial(finish, tile), out_shape=(jax.ShapeDtype...]
    pallas_call x1, Pallas kernels: 20.6 us -> 19.9 us  [on_device(): pl.pallas_call(functools.partial(kernel, rows, cols, tile, reach), out_sh...]
where the time goes in v2:
time: 23.2 us; the launch traced here: 23 us
  Pallas kernels  22.4 us (97%)
  between operations  0.64 us (3%)
    pallas_call x1, Pallas kernels, on_device(): pl.pallas_call(functools.partial(kernel, rows, cols, tile, reach), out_sh...  19.9 us
    pallas_call x1, Pallas kernels, on_device(): pl.pallas_call(functools.partial(finish, tile), out_shape=(jax.ShapeDtype...  2.47 us

profile of v2, /device:TPU:1, one launch (start us, length us, event | category | flops | bytes accessed | tf_op | source)
XLA Modules:
  0.0 23.0 jit_solution(987208942891301562)
XLA Ops:
  0.6 19.9 %shard_map.140 = (f32[4,4,128,128]{3,2,1,0:T(8,128)}, f32[128,128]{1,0:T(8,128)}, f32[128,128]{1,0:T(8,128)}, f32[2,4,4,128]{3,2,1,0:T(4,128)}) custom-call(f32[2,4,128,128]{3,2,1,0:T(8,128)} %em.1, f32[2,2,128,128]{3,2,1,0:T(8,128)} %wd.1, f32[65,4,65]{2,1,0:T(4,128)} %bitcast.1, f32[4,4,128,128]{3,2,1,0:T(8,128)} %bs.1, f32[4,4]{1,0:T(4,128)} %decay.1, ...), custom_call_target="tpu_custom_call" | custom-call | tf_op jit(solution)/shard_map/pallas_call | solution.py:439
  20.6 2.5 %shard_map.141 = (f32[4,4,128,128]{3,2,1,0:T(8,128)}, f32[4,128,128]{2,1,0:T(8,128)}) custom-call(f32[4,4,128,128]{3,2,1,0:T(8,128)} %get-tuple-element.6.part, f32[128,128]{1,0:T(8,128)} %get-tuple-element.7.side_halo, f32[128,128]{1,0:T(8,128)} %get-tuple-element.8.side_coef, f32[2,4,4,128]{3,2,1,0:T(4,128)} %get-tuple-element.9.row_halo), custom_call_target="tpu_custom_call" | custom-call | tf_op jit(solution)/shard_map/pallas_call | solution.py:488
